TPU v7x, 512 devices: a whole 4x8x8 slice. The times are simulated.
512 devices in a mesh: ctx: 64 (over x, y, core), tp: 8 (over z).
Axes of the slice: x: 4, y: 8, z: 8, core: 2. Of those that a mesh axis runs over, the one named last changes fastest.
Arguments:
- queries: bfloat16 [128, 2, 64, 128], P('ctx', None, 'tp'), may hold values from -64 to 64
- prefix_keys: bfloat16 [131072, 8, 128], P('ctx', 'tp'), may hold values from -8 to 8
- prefix_values: bfloat16 [131072, 8, 128], P('ctx', 'tp'), may hold values from -6 to 6
- suffix_keys: bfloat16 [128, 1024, 8, 128], P('ctx', None, 'tp'), may hold values from -8 to 8
- suffix_values: bfloat16 [128, 1024, 8, 128], P('ctx', None, 'tp'), may hold values from -6 to 6
- new_keys: bfloat16 [128, 2, 8, 128], P('ctx', None, 'tp'), may hold values from -12 to 12
- new_values: bfloat16 [128, 2, 8, 128], P('ctx', None, 'tp'), may hold values from -6 to 6
- suffix_lengths: int32 [128], P('ctx'), may hold values from 1 to 1024, 65536 in all
- out_weight: bfloat16 [8192, 8192], P('tp', 'ctx'), may hold values from -0.0625 to 0.0625
Outputs:
- projected: bfloat16 [128, 2, 8192], P('tp', None, 'ctx')
All inputs are finite; a program needn't handle non-finite values. No bound on the sum of `suffix_lengths` on one device may be relied on, other than what follows from the above.
Results may differ from a plain program's by a relative error of at most 0.02.
Values may be sent and summed in bfloat16 or wider, within the bound.
A program may use at most 192 MiB of HBM per device.

v0:
```python
import jax
import jax.numpy as jnp
from jax import lax
from jax.sharding import PartitionSpec as P

masked_score = -1e30


def block_samples(sample_count, per_sample):
    target = max(1, 512 // per_sample)
    chosen = 1
    for candidate in range(1, min(sample_count, target) + 1):
        if sample_count % candidate == 0:
            chosen = candidate
    return chosen


def joined(former, latter):
    former_top, former_total, former_weighted = former
    latter_top, latter_total, latter_weighted = latter
    row_top = jnp.maximum(former_top, latter_top)
    former_factor = jnp.exp(former_top - row_top)
    latter_factor = jnp.exp(latter_top - row_top)
    row_total = former_total * former_factor + latter_total * latter_factor
    weighted = (
        former_weighted * former_factor[..., None] + latter_weighted * latter_factor[..., None]
    )
    return (row_top, row_total, weighted)


def prefix_partial(every_query, prefix_keys, prefix_values, score_scale, group_size):
    sample_count, step_count, heads_loc, head_dim = every_query.shape
    kv_loc = heads_loc // group_size
    block_width = block_samples(sample_count, step_count * heads_loc)
    shaped = every_query.reshape(
        sample_count // block_width, block_width, step_count, kv_loc, group_size, head_dim
    )

    def attend_block(query_block):
        scores = (
            jnp.einsum(
                "stkgd,jkd->stkgj", query_block, prefix_keys, preferred_element_type=jnp.float32
            )
            * score_scale
        )
        row_top = jnp.max(scores, axis=-1)
        weights = jnp.exp(scores - row_top[..., None])
        row_total = jnp.sum(weights, axis=-1)
        weighted = jnp.einsum(
            "stkgj,jkd->stkgd",
            weights.astype(jnp.bfloat16),
            prefix_values,
            preferred_element_type=jnp.float32,
        )
        return (row_top, row_total, weighted)

    row_top, row_total, weighted = lax.map(attend_block, shaped)
    lead_shape = (sample_count, step_count, kv_loc, group_size)
    return (
        row_top.reshape(lead_shape),
        row_total.reshape(lead_shape),
        weighted.reshape(lead_shape + (head_dim,)),
    )


def recent_partial(
    queries,
    suffix_keys,
    suffix_values,
    new_keys,
    new_values,
    suffix_lengths,
    score_scale,
    group_size,
):
    samp_dev, step_count, heads_loc, head_dim = queries.shape
    kv_loc = heads_loc // group_size
    grouped = queries.reshape(samp_dev, step_count, kv_loc, group_size, head_dim)
    slot_count = suffix_keys.shape[1]
    live_slots = (jnp.arange(slot_count, dtype=jnp.int32)[None, :] < suffix_lengths[:, None])[
        :, None, None, None, :
    ]
    causal = (
        jnp.arange(step_count, dtype=jnp.int32)[:, None]
        >= jnp.arange(step_count, dtype=jnp.int32)[None, :]
    )[None, :, None, None, :]
    suffix_scores = (
        jnp.einsum("stkgd,sjkd->stkgj", grouped, suffix_keys, preferred_element_type=jnp.float32)
        * score_scale
    )
    suffix_scores = jnp.where(live_slots, suffix_scores, masked_score)
    recent_scores = (
        jnp.einsum("stkgd,sukd->stkgu", grouped, new_keys, preferred_element_type=jnp.float32)
        * score_scale
    )
    recent_scores = jnp.where(causal, recent_scores, masked_score)
    row_top = jnp.maximum(jnp.max(suffix_scores, axis=-1), jnp.max(recent_scores, axis=-1))
    suffix_weights = jnp.where(live_slots, jnp.exp(suffix_scores - row_top[..., None]), 0.0)
    recent_weights = jnp.where(causal, jnp.exp(recent_scores - row_top[..., None]), 0.0)
    row_total = jnp.sum(suffix_weights, axis=-1) + jnp.sum(recent_weights, axis=-1)
    weighted = jnp.einsum(
        "stkgj,sjkd->stkgd",
        suffix_weights.astype(jnp.bfloat16),
        suffix_values,
        preferred_element_type=jnp.float32,
    )
    weighted = weighted + jnp.einsum(
        "stkgu,sukd->stkgd",
        recent_weights.astype(jnp.bfloat16),
        new_values,
        preferred_element_type=jnp.float32,
    )
    return (row_top, row_total, weighted)


def per_device(
    queries,
    prefix_keys,
    prefix_values,
    suffix_keys,
    suffix_values,
    new_keys,
    new_values,
    suffix_lengths,
    out_weight,
):
    samp_dev, step_count, heads_loc, head_dim = queries.shape
    kv_loc = prefix_keys.shape[1]
    group_size = heads_loc // kv_loc
    score_scale = head_dim ** (-0.5)
    offset = lax.axis_index("ctx") * samp_dev
    every_query = lax.all_gather(queries, "ctx", axis=0, tiled=True)
    prefix_parts = prefix_partial(every_query, prefix_keys, prefix_values, score_scale, group_size)
    recent = recent_partial(
        queries,
        suffix_keys,
        suffix_values,
        new_keys,
        new_values,
        suffix_lengths,
        score_scale,
        group_size,
    )
    prefix_top, prefix_total, prefix_weighted = prefix_parts
    global_top = lax.pmax(prefix_top, "ctx")
    factor = jnp.exp(prefix_top - global_top)
    got_total, got_weighted = (
        lax.psum_scatter(prefix_total * factor, "ctx", scatter_dimension=0, tiled=True),
        lax.psum_scatter(
            prefix_weighted * factor[..., None], "ctx", scatter_dimension=0, tiled=True
        ),
    )
    own_top = lax.dynamic_slice_in_dim(global_top, offset, samp_dev, 0)
    row_top, row_total, weighted = joined((own_top, got_total, got_weighted), recent)
    attention = (weighted / row_total[..., None]).astype(jnp.bfloat16)
    attention = attention.reshape(samp_dev, step_count, heads_loc * head_dim)
    head_terms = jnp.einsum(
        "std,de->ste",
        lax.all_gather(attention, "ctx", axis=0, tiled=True),
        out_weight,
        preferred_element_type=jnp.float32,
    )
    return lax.psum_scatter(head_terms.astype(jnp.bfloat16), "tp", scatter_dimension=0, tiled=True)


def solution(mesh):
    placed = (
        P("ctx", None, "tp", None),
        P("ctx", "tp", None),
        P("ctx", "tp", None),
        P("ctx", None, "tp", None),
        P("ctx", None, "tp", None),
        P("ctx", None, "tp", None),
        P("ctx", None, "tp", None),
        P("ctx"),
        P("tp", "ctx"),
    )
    return jax.shard_map(
        per_device, mesh=mesh, in_specs=placed, out_specs=P("tp", None, "ctx"), check_vma=False
    )
```

profile of v0, /device:TPU:3, one launch (start us, length us, event | category | flops | bytes accessed | tf_op | source)
XLA Modules:
  0.0 664.5 jit_solution(4591430305079168251)
XLA Ops:
  6.5 0.0 copy-start
  6.5 0.0 reduce-scatter.4.cloned.1.call-start
  6.5 53.4 %all_gather.6 = bf16[128,2,8,128]{3,2,1,0:T(8,128)(2,1)S(1)} all-gather(bf16[2,2,8,128]{3,2,1,0:T(8,128)(2,1)} %param.11), channel_id=1, replica_groups=mesh['ctx'=64,'tp'=8] {'ctx'}, dimensions={0}, use_global_device_ids=true | all-gather | bytes 532480 | tf_op jit(solution)/shard_map/all_gather | solution.py:132
  60.0 14.4 %while.14 = (s32[]{:T(128)}, f32[4,32,2,1,8]{4,2,1,3,0:T(2,128)S(1)}, f32[4,32,2,1,8]{4,2,1,3,0:T(2,128)S(1)}, f32[4,32,2,1,8,128]{5,4,2,1,3,0:T(8,128)S(1)}, bf...) while((s32[]{:T(128)}, ...), condition=%wide.region_3.4_spmd, body=%wide.region_0.3_spmd.sunk | while | flops 545258496 | bytes 16291965 | solution.py:57
  60.0 0.0 copy-start.1
  60.0 1.9 bitcast_reduce_fusion.2
  61.9 0.8 fusion.67
  62.8 0.0 copy-done.1
  62.8 0.8 fusion.68
  63.6 0.0 copy-start.1
  63.6 1.9 bitcast_reduce_fusion.2
  65.5 0.8 fusion.67
  66.4 0.0 copy-done.1
  66.4 0.8 fusion.68
  67.2 0.0 copy-start.1
  67.2 1.9 bitcast_reduce_fusion.2
  69.1 0.8 fusion.67
  70.0 0.0 copy-done.1
  70.0 0.8 fusion.68
  70.8 0.0 copy-start.1
  70.8 1.9 bitcast_reduce_fusion.2
  72.7 0.8 fusion.67
  73.6 0.0 copy-done.1
  73.6 0.8 fusion.68
  74.4 0.0 copy-start.3
  74.4 0.0 copy-start.4
  74.4 0.0 copy-start.5
  74.4 0.0 copy-start.2
  74.4 0.0 copy-start.7
  74.4 0.0 copy-start.6
  74.4 208.2 %pmax.7 = f32[128,2,1,8]{3,1,0,2:T(2,128)S(1)} all-reduce(f32[128,2,1,8]{3,1,0,2:T(2,128)S(1)} %bitcast.199), channel_id=1, replica_groups=mesh['ctx'=64,'tp'=8] {'ctx'}, use_global_device_ids=true, to_apply=%region_4.5 | all-reduce | flops 2048 | bytes 16384 | tf_op jit(solution)/shard_map/pmax | solution.py:145
  282.7 0.1 fusion.42
  282.8 1.3 broadcast_multiply_fusion
  284.1 0.0 reduce-scatter.4.cloned.1.call-update
  284.2 0.0 reduce-scatter.6.cloned.1.call-start
  284.2 0.0 copy-done.3
  284.2 0.0 copy-done.4
  284.3 0.1 convolution_multiply_fusion.1
  284.4 246.3 %all-reduce = f32[128,2,1,8]{3,1,0,2:T(2,128)S(1)} all-reduce(f32[128,2,1,8]{3,1,0,2:T(2,128)S(1)} %get-tuple-element.81), channel_id=3, replica_groups=mesh['ctx'=64,'tp'=8] {'ctx'}, use_global_device_ids=true, to_apply=%region_8.9.clone | all-reduce | flops 2048 | bytes 16384
  530.7 1.3 dynamic-slice
  532.6 0.1 fusion.44
  532.7 0.0 copy-done.5
  532.7 0.1 iota_compare_fusion
  532.8 0.0 copy-done
  532.8 0.3 fusion.58
  533.1 0.2 fusion.35
  533.3 0.1 fusion.55
  533.5 0.0 copy-done.2
  533.5 0.2 fusion.30
  533.7 0.0 reduce-scatter.4.cloned.1.call-done
  533.7 0.0 copy-done.7
  533.8 0.9 fusion.29
  534.7 88.3 %all_gather.7 = bf16[128,2,1024]{2,1,0:T(2,128)(2,1)S(1)} all-gather(bf16[2,2,1024]{2,1,0:T(2,128)(2,1)S(1)} %reshape.180), channel_id=1, replica_groups=mesh['ctx'=64,'tp'=8] {'ctx'}, dimensions={0}, use_global_device_ids=true | all-gather | bytes 532480 | tf_op jit(solution)/shard_map/all_gather | solution.py:159
  623.0 0.0 copy-done.6
  623.0 0.9 convolution_convert_fusion
  623.9 0.0 reduce-scatter.6.cloned.1.call-update
  623.9 32.4 %reduce-scatter.6.cloned.1.call-done = bf16[16,2,128]{2,0,1:T(8,128)(2,1)} async-done(((bf16[128,2,128]{2,0,1:T(8,128)(2,1)}), bf16[16,2,128]{2,0,1:T(8,128)(2,1)}) %reduce-scatter.6.cloned.1.call-update) | async-done | bytes 8208 | tf_op jit(solution)/shard_map/reduce_scatter | solution.py:163
  656.4 1.3 copy.20
  (11 shorter events, 0.1 us)
Async XLA Ops:
  6.5 526.3 %copy-start = (bf16[2,1024,1,128]{3,1,2,0:T(8,128)(2,1)S(1)}, bf16[2,1024,1,128]{3,1,2,0:T(8,128)(2,1)}, u32[]{:S(2)}) copy-start(bf16[2,1024,1,128]{3,1,2,0:T(8,128)(2,1)} %param.14) | copy-start | bytes 1572868
  6.5 527.2 %reduce-scatter.4.cloned.1.call-start = ((), (), s32[]{:S(2)}) async-start(), calls=%async_computation.2 | async-start | bytes 1064960 | tf_op jit(solution)/shard_map/reduce_scatter | solution.py:149
  60.0 2.8 copy-start.1
  63.6 2.8 copy-start.1
  67.2 2.8 copy-start.1
  70.8 2.8 copy-start.1
  74.4 209.9 %copy-start.3 = (bf16[2,2,8,128]{3,2,1,0:T(8,128)(2,1)S(1)}, bf16[2,2,8,128]{3,2,1,0:T(8,128)(2,1)}, u32[]{:S(2)}) copy-start(bf16[2,2,8,128]{3,2,1,0:T(8,128)(2,1)} %param.11) | copy-start | bytes 24580
  74.4 209.9 %copy-start.4 = (bf16[2,2,1,128]{3,1,2,0:T(2,128)(2,1)S(1)}, bf16[2,2,1,128]{3,1,2,0:T(2,128)(2,1)}, u32[]{:S(2)}) copy-start(bf16[2,2,1,128]{3,1,2,0:T(2,128)(2,1)} %param.16) | copy-start | bytes 3076
  74.4 458.3 %copy-start.5 = (s32[2]{0:T(128)S(1)}, s32[2]{0:T(128)}, u32[]{:S(2)}) copy-start(s32[2]{0:T(128)} %param.18) | copy-start | bytes 28
  74.4 459.1 %copy-start.2 = (bf16[2,1024,1,128]{3,1,2,0:T(8,128)(2,1)S(1)}, bf16[2,1024,1,128]{3,1,2,0:T(8,128)(2,1)}, u32[]{:S(2)}) copy-start(bf16[2,1024,1,128]{3,1,2,0:T(8,128)(2,1)} %param.15) | copy-start | bytes 1572868
  74.4 459.3 %copy-start.7 = (bf16[2,2,1,128]{3,1,2,0:T(2,128)(2,1)S(1)}, bf16[2,2,1,128]{3,1,2,0:T(2,128)(2,1)}, u32[]{:S(2)}) copy-start(bf16[2,2,1,128]{3,1,2,0:T(2,128)(2,1)} %param.17) | copy-start | bytes 3076
  74.4 548.6 %copy-start.6 = (bf16[1024,128]{1,0:T(8,128)(2,1)S(1)}, bf16[1024,128]{1,0:T(8,128)(2,1)}, u32[]{:S(2)}) copy-start(bf16[1024,128]{1,0:T(8,128)(2,1)} %param.19) | copy-start | bytes 786436
  284.2 372.2 %reduce-scatter.6.cloned.1.call-start = ((), (), s32[]{:S(2)}) async-start(), calls=%async_computation.3 | async-start | bytes 73728 | tf_op jit(solution)/shard_map/reduce_scatter | solution.py:163
Sparse Core Ops, SparseCore 0:
  284.3 177.0 reduce-scatter.3
  624.1 32.2 reduce-scatter.5
where the time goes:
time: 670 us; the launch traced here: 664 us
  blocking collectives  596 us (89%)
  waiting for transfers between devices  32.5 us (5%)
  between operations  14.2 us (2%)
  matrix products  13.3 us (2%)
    unnamed x1, blocking collectives  246 us
    pmax x1, blocking collectives, per_device(): global_top = lax.pmax(prefix_top, 'ctx')  208 us
    all_gather x1, blocking collectives, per_device(): lax.all_gather(attention, 'ctx', axis=0, tiled=True)  88.3 us
    all_gather x1, blocking collectives, per_device(): every_query = lax.all_gather(queries, 'ctx', axis=0, tiled=True)  53.4 us
    reduce_scatter x1, waiting for transfers between devices, per_device(): lax.psum_scatter(head_terms.astype(jnp.bfloat16), 'tp', scatter_dimension...  32.4 us
  transfers between devices with their start and end apart: 2, of which 1 were waited for; matrix products, arithmetic and copies ran while one was open for 0% of the time, Pallas kernels for 0%

commit v1 on v0

v1 whole, which is shorter than its diff:
```python
import functools
import math

import jax
import jax.numpy as jnp
from jax import lax
from jax.experimental import pallas as pl
from jax.experimental.pallas import tpu as pltpu
from jax.sharding import PartitionSpec as P

MESH = pl.DeviceIdType.MESH
LANES = 128
CORES = 2
masked_score = -1e30


def dot_rows(left, right):
    return lax.dot_general(
        left, right, (((1,), (1,)), ((), ())), preferred_element_type=jnp.float32
    )


def attend_kernel(
    sizes,
    q_ref,
    k_ref,
    v_ref,
    sk_ref,
    sv_ref,
    nk_ref,
    nv_ref,
    len_ref,
    w_ref,
    out_ref,
    kbuf,
    vbuf,
    skbuf,
    svbuf,
    nkbuf,
    nvbuf,
    wbuf,
    qbuf,
    parts,
    part_tops,
    sib_parts,
    sib_tops,
    merged,
    merged_tops,
    x_parts,
    x_tops,
    y_send,
    y_send_tops,
    y_parts,
    y_tops,
    suffix_part,
    suffix_top,
    abuf,
    attention32,
    z_send,
    z_parts,
    local_sem,
    send_sem,
    recv_sem,
    z_send_sem,
    z_recv_sem,
):
    nx, ny, nz = sizes
    rows = q_ref.shape[0]
    chunk = ny * rows
    stat_rows = chunk // LANES
    groups = LANES // rows
    head_dim = q_ref.shape[1]
    samp_dev, slots = sk_ref.shape[0], sk_ref.shape[1]
    samp_rows = rows // samp_dev
    steps = nk_ref.shape[1]
    heads = samp_rows // steps
    log2_scale = (head_dim ** (-0.5)) * math.log2(math.e)

    me = lax.axis_index("ctx")
    z0 = lax.axis_index("tp")
    c0 = lax.rem(me, CORES)
    y0 = lax.rem(lax.div(me, CORES), ny)
    x0 = lax.div(me, CORES * ny)

    def at(x, y, c):
        return {"ctx": (x * ny + y) * CORES + c}

    def x_plus(d):
        return lax.rem(x0 + d, nx)

    def y_plus(d):
        return lax.rem(y0 + d, ny)

    sibling = at(x0, y0, 1 - c0)
    cother = 1 - c0

    bases = {}
    count = 0
    for name, amount in (
        ("qy", ny),
        ("qx", nx),
        ("qc", nx),
        ("pc", nx),
        ("pct", nx),
        ("px", nx),
        ("pxt", nx),
        ("py", ny),
        ("pyt", ny),
        ("ay", ny),
        ("ax", nx),
        ("ac", nx),
    ):
        bases[name] = count
        count += amount

    def remote(name, d, src, dst, device):
        slot = bases[name] + d
        return pltpu.make_async_remote_copy(
            src_ref=src,
            dst_ref=dst,
            send_sem=send_sem.at[slot],
            recv_sem=recv_sem.at[slot],
            device_id=device,
            device_id_type=MESH,
        )

    def q_y(d):
        return remote("qy", d, q_ref, qbuf.at[x0, c0, y0], at(x0, y_plus(d), c0))

    def q_x(d):
        return remote("qx", d, qbuf.at[x0, c0], qbuf.at[x0, c0], at(x_plus(d), y0, c0))

    def q_core(dx):
        x = x_plus(dx)
        return remote("qc", dx, qbuf.at[x, c0], qbuf.at[x, c0], sibling)

    def p_core(dx):
        return remote("pc", dx, parts.at[1, dx], sib_parts.at[dx], sibling)

    def pt_core(dx):
        return remote("pct", dx, part_tops.at[1, dx], sib_tops.at[dx], sibling)

    def p_x(dx):
        return remote("px", dx, merged.at[dx], x_parts.at[dx], at(x_plus(dx), y0, c0))

    def pt_x(dx):
        return remote("pxt", dx, merged_tops.at[dx], x_tops.at[dx], at(x_plus(dx), y0, c0))

    def p_y(d):
        y = y_plus(d)
        return remote("py", d, y_send.at[y], y_parts.at[y0], at(x0, y, c0))

    def pt_y(d):
        y = y_plus(d)
        return remote(
            "pyt",
            d,
            y_send_tops.at[(-d) % groups, lax.div(y, groups)],
            y_tops.at[y0],
            at(x0, y, c0),
        )

    def a_y(d):
        mine = abuf.at[x0, y0, c0]
        return remote("ay", d, mine, mine, at(x0, y_plus(d), c0))

    def a_x(d):
        mine = abuf.at[x0, :, c0]
        return remote("ax", d, mine, mine, at(x_plus(d), y0, c0))

    def a_core(dx):
        mine = abuf.at[x_plus(dx), :, c0]
        return remote("ac", dx, mine, mine, sibling)

    def z_copy(dx, j):
        z = x_plus(dx) * (nz // nx) + j
        d = lax.rem(z - z0 + nz, nz)
        return z, pltpu.make_async_remote_copy(
            src_ref=z_send.at[dx, j],
            dst_ref=z_parts.at[z0],
            send_sem=z_send_sem.at[dx, j],
            recv_sem=z_recv_sem.at[d],
            device_id={"tp": z},
            device_id_type=MESH,
        )

    barrier = pltpu.get_barrier_semaphore()
    partners = [at(x0, y_plus(d), c0) for d in range(1, ny)]
    partners += [at(x_plus(d), y0, c0) for d in range(1, nx)]
    partners += [sibling]
    partners += [{"tp": lax.rem(z0 + d, nz)} for d in range(1, nz)]
    for partner in partners:
        pl.semaphore_signal(barrier, inc=1, device_id=partner, device_id_type=MESH)

    local = [
        pltpu.make_async_copy(q_ref, qbuf.at[x0, c0, y0], local_sem.at[0]),
        pltpu.make_async_copy(sk_ref, skbuf, local_sem.at[1]),
        pltpu.make_async_copy(nk_ref, nkbuf, local_sem.at[2]),
        pltpu.make_async_copy(nv_ref, nvbuf, local_sem.at[3]),
        pltpu.make_async_copy(sv_ref, svbuf, local_sem.at[4]),
        pltpu.make_async_copy(k_ref, kbuf, local_sem.at[5]),
        pltpu.make_async_copy(v_ref, vbuf.at[:, 0:head_dim], local_sem.at[6]),
        pltpu.make_async_copy(w_ref, wbuf, local_sem.at[7]),
    ]
    for copy in local:
        copy.start()
    vbuf[:, head_dim:] = jnp.ones((vbuf.shape[0], LANES), jnp.bfloat16)

    pl.semaphore_wait(barrier, len(partners))
    order = sorted(range(1, ny), key=lambda d: -min(d, ny - d))
    for d in order:
        q_y(d).start()

    for copy in local[:5]:
        copy.wait()
    own_queries = qbuf[x0, c0, y0]
    row_in_sample = lax.broadcasted_iota(jnp.int32, (samp_rows, 1), 0)
    slot_index = lax.broadcasted_iota(jnp.int32, (samp_rows, slots), 1)
    outs, tops = [], []
    for s in range(samp_dev):
        queries = own_queries[s * samp_rows : (s + 1) * samp_rows]
        scores = dot_rows(queries, skbuf[s])
        scores = jnp.where(slot_index < len_ref[s], scores, masked_score)
        new_keys = nkbuf[s].astype(jnp.float32)
        new_values = nvbuf[s].astype(jnp.float32)
        row_top = jnp.max(scores, axis=1, keepdims=True)
        recent = []
        for u in range(steps):
            score = jnp.sum(
                queries.astype(jnp.float32) * new_keys[u : u + 1], axis=1, keepdims=True
            )
            score = jnp.where(row_in_sample >= u * heads, score, masked_score)
            row_top = jnp.maximum(row_top, score)
            recent.append(score)
        weights = jnp.exp2((scores - row_top) * log2_scale)
        row_total = jnp.sum(weights, axis=1, keepdims=True)
        weighted = jnp.dot(
            weights.astype(jnp.bfloat16), svbuf[s], preferred_element_type=jnp.float32
        )
        for u in range(steps):
            weight = jnp.exp2((recent[u] - row_top) * log2_scale)
            row_total = row_total + weight
            weighted = weighted + weight.astype(jnp.bfloat16).astype(jnp.float32) * (
                new_values[u : u + 1]
            )
        suffix_part[s * samp_rows : (s + 1) * samp_rows, :] = weighted / row_total
        outs.append(row_top * log2_scale + jnp.log2(row_total))
    lane = lax.broadcasted_iota(jnp.int32, (rows, LANES), 1)
    sub = lax.broadcasted_iota(jnp.int32, (rows, LANES), 0)
    suffix_top[...] = jnp.sum(
        jnp.where(lax.rem(lane, rows) == sub, jnp.concatenate(outs, axis=0), 0.0),
        axis=0,
        keepdims=True,
    )

    for d in range(1, ny):
        q_y(d).wait_recv()
    q_core(0).start()
    for d in range(1, nx):
        q_x(d).start()
    local[5].wait()
    local[6].wait()

    eye = lax.broadcasted_iota(jnp.int32, (LANES, LANES), 0) == lax.broadcasted_iota(
        jnp.int32, (LANES, LANES), 1
    )

    def attend(queries):
        scores = dot_rows(queries, kbuf[...])
        row_top = jnp.max(scores, axis=1, keepdims=True)
        weights = jnp.exp2((scores - row_top) * log2_scale).astype(jnp.bfloat16)
        both = jnp.dot(weights, vbuf[...], preferred_element_type=jnp.float32)
        total = both[:, head_dim:]
        part = (both[:, :head_dim] / total).astype(jnp.bfloat16)
        return part, row_top * log2_scale + jnp.log2(total)

    def combine(sources):
        top = sources[0][1]
        for _, stat in sources[1:]:
            top = jnp.maximum(top, stat)
        weights = [jnp.exp2(stat - top) for _, stat in sources]
        total = sum(weights[1:], weights[0])
        inverse = 1.0 / total
        joined_top = top + jnp.log2(total)
        joined = []
        for g in range(stat_rows):
            result = None
            for (read, _), weight in zip(sources, weights):
                spread = jnp.where(eye, (weight * inverse)[g : g + 1], 0.0)
                term = jnp.dot(
                    spread.astype(jnp.bfloat16), read(g), preferred_element_type=jnp.float32
                )
                result = term if result is None else result + term
            joined.append(result.astype(jnp.bfloat16))
        return joined, joined_top

    def reader(ref, *index):
        return lambda g: ref[(*index, pl.ds(g * LANES, LANES))]

    def stats(ref, *index):
        return ref[index][0:stat_rows]

    def merge_pair(dx):
        p_core(dx).wait_recv()
        pt_core(dx).wait_recv()
        joined, top = combine(
            [
                (reader(parts, 0, dx), stats(part_tops, 0, dx)),
                (reader(sib_parts, dx), stats(sib_tops, dx)),
            ]
        )
        for g in range(stat_rows):
            merged[dx, pl.ds(g * LANES, LANES)] = joined[g]
        merged_tops[dx, 0:stat_rows] = top
        p_x(dx).start()
        pt_x(dx).start()

    last = 2 * nx - 1

    def step(i, carry):
        dx = lax.rem(lax.div(i + 1, 2), nx)
        flag = lax.rem(i, 2) + lax.div(last - i, last) - lax.div(i, last)
        for k in range(1, nx):

            @pl.when(i == 2 * k - 1)
            def _():
                for ahead in range(1, nx) if k == 1 else ():
                    q_x(nx - ahead).wait_recv()
                    q_core(ahead).start()
                q_core(k).wait_recv()

        @pl.when(i == 0)
        def _():
            q_core(0).wait_recv()

        queries = qbuf[x_plus(dx), lax.rem(c0 + flag, CORES)].reshape(chunk, head_dim)
        part, top = attend(queries)
        parts[flag, dx] = part
        for g in range(stat_rows):
            part_tops[flag, dx, g : g + 1] = jnp.sum(
                jnp.where(eye, top[g * LANES : (g + 1) * LANES], 0.0), axis=0, keepdims=True
            )

        for k in range(nx):

            @pl.when(i == max(2 * k - 1, 0))
            def _():
                p_core(k).start()
                pt_core(k).start()

        for k in range(1, nx):

            @pl.when(i == 2 * k)
            def _():
                merge_pair(k)

        return carry

    part_tops[...] = jnp.zeros_like(part_tops)
    merged_tops[...] = jnp.zeros_like(merged_tops)
    lax.fori_loop(0, 2 * nx, step, 0)

    p_core(0).wait_recv()
    pt_core(0).wait_recv()
    sources = [
        (reader(parts, 0, 0), stats(part_tops, 0, 0)),
        (reader(sib_parts, 0), stats(sib_tops, 0)),
    ]
    for d in range(1, nx):
        p_x(d).wait_recv()
        pt_x(d).wait_recv()
        sources.append((reader(x_parts, d), stats(x_tops, d)))
    joined, top = combine(sources)
    per_group = LANES // rows
    for g in range(stat_rows):
        for j in range(per_group):
            y_send[g * per_group + j] = joined[g][j * rows : (j + 1) * rows]
    for turn in range(groups):
        turned = pltpu.roll(top, turn * rows, 1) if turn else top
        for g in range(stat_rows):
            y_send_tops[turn, g] = turned[g : g + 1]
    for d in order:
        p_y(d).start()
        pt_y(d).start()
    y_parts[y0] = y_send[y0]
    y_tops[y0] = y_send_tops[0, lax.div(y0, groups)]
    for d in range(1, ny):
        p_y(d).wait_recv()
        pt_y(d).wait_recv()

    lane_row = lax.broadcasted_iota(jnp.int32, (1, LANES), 1)
    flat = []
    for g in range(stat_rows):
        line = jnp.zeros((1, LANES), jnp.float32)
        for j in range(groups):
            line = jnp.where(lax.div(lane_row, rows) == j, y_tops[g * groups + j], line)
        flat.append(line)

    def over_groups(lines, op):
        result = functools.reduce(op, lines)
        turn = LANES // 2
        while turn >= rows:
            result = op(result, pltpu.roll(result, turn, 1))
            turn //= 2
        return result

    own_top = suffix_top[...]
    row_top = jnp.maximum(over_groups(flat, jnp.maximum), own_top)
    flat = [jnp.exp2(line - row_top) for line in flat]
    own_weight = jnp.exp2(own_top - row_top)
    inverse = 1.0 / (over_groups(flat, jnp.add) + own_weight)
    own_column = jnp.sum(
        jnp.where(lane == sub, own_weight * inverse, 0.0), axis=1, keepdims=True
    )
    result = own_column * suffix_part[...]
    for g in range(stat_rows):
        spread = jnp.where(lax.rem(lane, rows) == sub, flat[g] * inverse, 0.0)
        result = result + jnp.dot(
            spread.astype(jnp.bfloat16),
            y_parts[g * groups : (g + 1) * groups].reshape(LANES, head_dim),
            preferred_element_type=jnp.float32,
        )
    abuf[x0, y0, c0] = result.astype(jnp.bfloat16)

    for d in order:
        a_y(d).start()
    for d in range(1, ny):
        a_y(d).wait_recv()
    for d in range(1, nx):
        a_x(d).start()
    a_core(0).start()
    local[7].wait()

    tokens = chunk * CORES // heads
    share = tokens * nx // nz

    def project(dx):
        a_core(dx).wait_recv()
        attention32[...] = (
            abuf[x_plus(dx)].reshape(chunk * CORES, head_dim).astype(jnp.float32)
        )
        features = jnp.concatenate(
            [
                attention32[pl.ds(h, tokens, stride=heads), :].astype(jnp.bfloat16)
                for h in range(heads)
            ],
            axis=1,
        )
        terms = jnp.dot(features, wbuf[...], preferred_element_type=jnp.float32)
        terms = terms.astype(jnp.bfloat16)
        for j in range(nz // nx):
            z_send[dx, j] = terms[j * share : (j + 1) * share]
            z, copy = z_copy(dx, j)

            @pl.when(z != z0)
            def _():
                copy.start()

            @pl.when(z == z0)
            def _():
                z_parts[z0] = z_send[dx, j]

    project(0)
    for dx in range(1, nx):
        a_x(nx - dx).wait_recv()
        a_core(dx).start()
    for dx in range(1, nx):
        project(dx)

    for d in range(1, nz):
        pltpu.make_async_remote_copy(
            src_ref=z_send.at[0, 0],
            dst_ref=z_parts.at[0],
            send_sem=z_send_sem.at[0, 0],
            recv_sem=z_recv_sem.at[d],
            device_id={"tp": z0},
            device_id_type=MESH,
        ).wait_recv()
    total = z_parts[0].astype(jnp.float32)
    for z in range(1, nz):
        total = total + z_parts[z].astype(jnp.float32)
    out_ref[...] = total.astype(jnp.bfloat16)

    for d in range(1, ny):
        for copy in (q_y, p_y, pt_y, a_y):
            copy(d).wait_send()
    for d in range(1, nx):
        for copy in (q_x, p_x, pt_x, a_x):
            copy(d).wait_send()
    for dx in range(nx):
        for copy in (q_core, p_core, pt_core, a_core):
            copy(dx).wait_send()
        for j in range(nz // nx):
            z, copy = z_copy(dx, j)

            @pl.when(z != z0)
            def _():
                copy.wait_send()


def per_device(
    sizes,
    queries,
    prefix_keys,
    prefix_values,
    suffix_keys,
    suffix_values,
    new_keys,
    new_values,
    suffix_lengths,
    out_weight,
):
    nx, ny, nz = sizes
    samp_dev, steps, heads, head_dim = queries.shape
    rows = samp_dev * steps * heads
    chunk = ny * rows
    keys = prefix_keys.shape[0]
    slots = suffix_keys.shape[1]
    columns = out_weight.shape[1]
    tokens = chunk * CORES // heads
    share = tokens * nx // nz
    groups = LANES // rows
    stat_rows = chunk // LANES
    bf16, f32 = jnp.bfloat16, jnp.float32
    sems = 5 * ny + 7 * nx
    anywhere = pl.BlockSpec(memory_space=pl.ANY)
    out = pl.pallas_call(
        functools.partial(attend_kernel, sizes),
        out_shape=jax.ShapeDtypeStruct((share, columns), bf16),
        in_specs=[anywhere] * 7 + [pl.BlockSpec(memory_space=pltpu.SMEM), anywhere],
        out_specs=pl.BlockSpec(memory_space=pltpu.VMEM),
        scratch_shapes=[
            pltpu.VMEM((keys, head_dim), bf16),
            pltpu.VMEM((keys, head_dim + LANES), bf16),
            pltpu.VMEM((samp_dev, slots, head_dim), bf16),
            pltpu.VMEM((samp_dev, slots, head_dim), bf16),
            pltpu.VMEM((samp_dev, steps, head_dim), bf16),
            pltpu.VMEM((samp_dev, steps, head_dim), bf16),
            pltpu.VMEM((heads * head_dim, columns), bf16),
            pltpu.VMEM((nx, CORES, ny, rows, head_dim), bf16),
            pltpu.VMEM((2, nx, chunk, head_dim), bf16),
            pltpu.VMEM((2, nx, 8, LANES), f32),
            pltpu.VMEM((nx, chunk, head_dim), bf16),
            pltpu.VMEM((nx, 8, LANES), f32),
            pltpu.VMEM((nx, chunk, head_dim), bf16),
            pltpu.VMEM((nx, 8, LANES), f32),
            pltpu.VMEM((nx, chunk, head_dim), bf16),
            pltpu.VMEM((nx, 8, LANES), f32),
            pltpu.VMEM((ny, rows, head_dim), bf16),
            pltpu.VMEM((groups, stat_rows, 1, LANES), f32),
            pltpu.VMEM((ny, rows, head_dim), bf16),
            pltpu.VMEM((ny, 1, LANES), f32),
            pltpu.VMEM((rows, head_dim), f32),
            pltpu.VMEM((1, LANES), f32),
            pltpu.VMEM((nx, ny, CORES, rows, head_dim), bf16),
            pltpu.VMEM((chunk * CORES, head_dim), f32),
            pltpu.VMEM((nx, nz // nx, share, columns), bf16),
            pltpu.VMEM((nz, share, columns), bf16),
            pltpu.SemaphoreType.DMA((8,)),
            pltpu.SemaphoreType.DMA((sems,)),
            pltpu.SemaphoreType.DMA((sems,)),
            pltpu.SemaphoreType.DMA((nx, nz // nx)),
            pltpu.SemaphoreType.DMA((nz,)),
        ],
        compiler_params=pltpu.CompilerParams(
            collective_id=0, has_side_effects=True, vmem_limit_bytes=40 * 1024 * 1024
        ),
    )(
        queries.reshape(rows, head_dim),
        prefix_keys.reshape(keys, head_dim),
        prefix_values.reshape(keys, head_dim),
        suffix_keys.reshape(samp_dev, slots, head_dim),
        suffix_values.reshape(samp_dev, slots, head_dim),
        new_keys.reshape(samp_dev, steps, head_dim),
        new_values.reshape(samp_dev, steps, head_dim),
        suffix_lengths,
        out_weight,
    )
    return out.reshape(share // steps, steps, columns)


def solution(mesh, sizes=(4, 8, 8)):
    placed = (
        P("ctx", None, "tp", None),
        P("ctx", "tp", None),
        P("ctx", "tp", None),
        P("ctx", None, "tp", None),
        P("ctx", None, "tp", None),
        P("ctx", None, "tp", None),
        P("ctx", None, "tp", None),
        P("ctx"),
        P("tp", "ctx"),
    )
    return jax.shard_map(
        functools.partial(per_device, sizes),
        mesh=mesh,
        in_specs=placed,
        out_specs=P("tp", None, "ctx"),
        check_vma=False,
    )
```

time: 670 us -> 64.9 us (0.10)
  blocking collectives: 596 us -> 0 us
  Pallas kernels: 0 us -> 58 us
  waiting for transfers between devices: 32.5 us -> 0 us
  between operations: 14.2 us -> 0.03 us
  matrix products: 13.3 us -> 0 us
    unnamed x1 -> x0, blocking collectives: 246 us -> none
    pmax x1 -> x0, blocking collectives: 208 us -> none  [per_device(): global_top = lax.pmax(prefix_top, 'ctx')]
    all_gather x2 -> x0, blocking collectives: 142 us -> none  [the longest x1 88.3 us: per_device(): lax.all_gather(attention, 'ctx', axis=0, tiled=True)]
    pallas_call x0 -> x1, Pallas kernels: none -> 58 us  [per_device(): pl.pallas_call(functools.partial(attend_kernel, sizes), out_shape=jax.Sha...]
    reduce_scatter x2 -> x0, waiting for transfers between devices: 32.4 us -> none  [the longest x1 32.4 us: per_device(): lax.psum_scatter(head_terms.astype(jnp.bfloat16), 'tp', scatter_dimension...]
    dot_general x13 -> x0, matrix products: 13.3 us -> none  [the longest x4 7.64 us: attend_block(): jnp.einsum('stkgd,jkd->stkgj', query_block, prefix_keys, preferred_elemen...]
  transfers between devices with their start and end apart: 2 -> 0, of which waited for: 1 -> 0; matrix products, arithmetic and copies ran while one was open for 0% -> 0% of each run, Pallas kernels for 0% -> 0%
where the time goes in v1:
time: 64.9 us; the launch traced here: 64.5 us
  Pallas kernels  58 us (89%)
  local copies, waits for them, and re-layouts  6.41 us (10%)
    pallas_call x1, Pallas kernels, per_device(): pl.pallas_call(functools.partial(attend_kernel, sizes), out_shape=jax.Sha...  58 us
    unnamed x19, local copies, waits for them, and re-layouts  6.41 us

profile of v1, /device:TPU:3, one launch (start us, length us, event | category | flops | bytes accessed | tf_op | source)
XLA Modules:
  0.0 64.5 jit_solution(10282808561486496688)
XLA Ops:
  0.0 0.0 copy-start.5
  0.0 0.0 copy-start.7
  0.0 0.0 copy-start.6
  0.0 0.0 copy-start.8
  0.0 0.7 %copy-done.5 = bf16[2,2,8,128]{3,2,1,0:T(8,128)(2,1)S(1)} copy-done((bf16[2,2,8,128]{3,2,1,0:T(8,128)(2,1)S(1)}, bf16[2,2,8,128]{3,2,1,0:T(8,128)(2,1)}, u32[]{:S(2)}) %copy-start.5) | copy-done | bytes 8216
  0.7 0.0 copy-done.7
  0.7 0.0 copy-done.6
  0.7 0.0 copy-done.8
  0.7 0.0 copy-start
  0.7 1.0 %copy-done = bf16[2048,1,128]{2,0,1:T(8,128)(2,1)S(1)} copy-done((bf16[2048,1,128]{2,0,1:T(8,128)(2,1)S(1)}, bf16[2048,1,128]{2,0,1:T(8,128)(2,1)}, u32[]{:S(2)}) %copy-start) | copy-done | bytes 524312
  1.8 0.0 copy-start.1
  1.8 1.0 %copy-done.1 = bf16[2048,1,128]{2,0,1:T(8,128)(2,1)S(1)} copy-done((bf16[2048,1,128]{2,0,1:T(8,128)(2,1)S(1)}, bf16[2048,1,128]{2,0,1:T(8,128)(2,1)}, u32[]{:S(2)}) %copy-start.1) | copy-done | bytes 524312
  2.8 0.0 copy-start.2
  2.8 1.0 %copy-done.2 = bf16[2,1024,1,128]{3,1,2,0:T(8,128)(2,1)S(1)} copy-done((bf16[2,1024,1,128]{3,1,2,0:T(8,128)(2,1)S(1)}, bf16[2,1024,1,128]{3,1,2,0:T(8,128)(2,1)}, u32[]{:S(2)}) %copy-start.2) | copy-done | bytes 524312
  3.8 0.0 copy-start.3
  3.8 1.0 %copy-done.3 = bf16[2,1024,1,128]{3,1,2,0:T(8,128)(2,1)S(1)} copy-done((bf16[2,1024,1,128]{3,1,2,0:T(8,128)(2,1)S(1)}, bf16[2,1024,1,128]{3,1,2,0:T(8,128)(2,1)}, u32[]{:S(2)}) %copy-start.3) | copy-done | bytes 524312
  4.9 0.0 copy-start.4
  4.9 0.9 %copy-done.4 = bf16[1024,128]{1,0:T(8,128)(2,1)S(1)} copy-done((bf16[1024,128]{1,0:T(8,128)(2,1)S(1)}, bf16[1024,128]{1,0:T(8,128)(2,1)}, u32[]{:S(2)}) %copy-start.4) | copy-done | bytes 262168
  5.8 58.0 %shard_map.91 = bf16[32,128]{1,0:T(8,128)(2,1)S(1)} custom-call(bf16[32,128]{1,0:T(8,128)(2,1)S(1)} %bitcast.13, bf16[2048,128]{1,0:T(8,128)(2,1)S(1)} %bitcast.8, bf16[2048,128]{1,0:T(8,128)(2,1)S(1)} %bitcast.9, bf16[2,1024,128]{2,1,0:T(8,128)(2,1)S(1)} %bitcast.10, bf16[2,1024,128]{2,1,0:T(8,128)(2,1)S(1)} %bitcast.11, bf16[2,2,128]{2,1,0:T(2,128)(2,1)S(1)} %bitcast.14, ...), custom_call_target="tpu_custom_call" | custom-call | tf_op jit(solution)/shard_map/pallas_call | solution.py:527
  63.9 0.6 copy.11
Async XLA Ops:
  0.0 0.7 %copy-start.5 = (bf16[2,2,8,128]{3,2,1,0:T(8,128)(2,1)S(1)}, bf16[2,2,8,128]{3,2,1,0:T(8,128)(2,1)}, u32[]{:S(2)}) copy-start(bf16[2,2,8,128]{3,2,1,0:T(8,128)(2,1)} %param.9) | copy-start | bytes 24580
  0.0 0.7 %copy-start.7 = (bf16[2,2,1,128]{3,1,2,0:T(2,128)(2,1)S(1)}, bf16[2,2,1,128]{3,1,2,0:T(2,128)(2,1)}, u32[]{:S(2)}) copy-start(bf16[2,2,1,128]{3,1,2,0:T(2,128)(2,1)} %param.15) | copy-start | bytes 3076
  0.0 0.7 %copy-start.6 = (bf16[2,2,1,128]{3,1,2,0:T(2,128)(2,1)S(1)}, bf16[2,2,1,128]{3,1,2,0:T(2,128)(2,1)}, u32[]{:S(2)}) copy-start(bf16[2,2,1,128]{3,1,2,0:T(2,128)(2,1)} %param.14) | copy-start | bytes 3076
  0.0 0.7 %copy-start.8 = (s32[2]{0:T(128)S(1)}, s32[2]{0:T(128)}, u32[]{:S(2)}) copy-start(s32[2]{0:T(128)} %len_ref.1) | copy-start | bytes 28
  0.7 1.0 %copy-start = (bf16[2048,1,128]{2,0,1:T(8,128)(2,1)S(1)}, bf16[2048,1,128]{2,0,1:T(8,128)(2,1)}, u32[]{:S(2)}) copy-start(bf16[2048,1,128]{2,0,1:T(8,128)(2,1)} %param.10) | copy-start | bytes 1572868
  1.8 1.0 %copy-start.1 = (bf16[2048,1,128]{2,0,1:T(8,128)(2,1)S(1)}, bf16[2048,1,128]{2,0,1:T(8,128)(2,1)}, u32[]{:S(2)}) copy-start(bf16[2048,1,128]{2,0,1:T(8,128)(2,1)} %param.11) | copy-start | bytes 1572868
  2.8 1.0 %copy-start.2 = (bf16[2,1024,1,128]{3,1,2,0:T(8,128)(2,1)S(1)}, bf16[2,1024,1,128]{3,1,2,0:T(8,128)(2,1)}, u32[]{:S(2)}) copy-start(bf16[2,1024,1,128]{3,1,2,0:T(8,128)(2,1)} %param.12) | copy-start | bytes 1572868
  3.8 1.0 %copy-start.3 = (bf16[2,1024,1,128]{3,1,2,0:T(8,128)(2,1)S(1)}, bf16[2,1024,1,128]{3,1,2,0:T(8,128)(2,1)}, u32[]{:S(2)}) copy-start(bf16[2,1024,1,128]{3,1,2,0:T(8,128)(2,1)} %param.13) | copy-start | bytes 1572868
  4.9 0.9 %copy-start.4 = (bf16[1024,128]{1,0:T(8,128)(2,1)S(1)}, bf16[1024,128]{1,0:T(8,128)(2,1)}, u32[]{:S(2)}) copy-start(bf16[1024,128]{1,0:T(8,128)(2,1)} %w_ref.1) | copy-start | bytes 786436

commit v2 on v1

v2 whole, which is shorter than its diff:
```python
import functools
import math

import jax
import jax.numpy as jnp
from jax import lax
from jax.experimental import pallas as pl
from jax.experimental.pallas import tpu as pltpu
from jax.sharding import PartitionSpec as P

MESH = pl.DeviceIdType.MESH
LANES = 128
CORES = 2
masked_score = -1e30


def dot_rows(left, right):
    return lax.dot_general(
        left, right, (((1,), (1,)), ((), ())), preferred_element_type=jnp.float32
    )


def dot(left, right):
    return jnp.dot(left, right, preferred_element_type=jnp.float32)


def attend_kernel(
    sizes,
    q_ref,
    k_ref,
    v_ref,
    sk_ref,
    sv_ref,
    nk_ref,
    nv_ref,
    len_ref,
    w_ref,
    out_ref,
    kbuf,
    vbuf,
    skbuf,
    svbuf,
    nkbuf,
    nvbuf,
    wbuf,
    qbuf,
    parts,
    part_tops,
    y_parts,
    y_tops,
    merged,
    merged_top,
    x_parts,
    x_tops,
    suffix_part,
    suffix_top,
    abuf,
    attention32,
    z_send,
    z_parts,
    local_sem,
    send_sem,
    recv_sem,
    qy_sem,
):
    nx, ny, nz = sizes
    rows, head_dim = q_ref.shape
    samp_dev, slots = sk_ref.shape[0], sk_ref.shape[1]
    keys = k_ref.shape[0]
    samp_rows = rows // samp_dev
    steps = nk_ref.shape[1]
    heads = samp_rows // steps
    tokens = rows // heads
    line = nx * rows
    log2_scale = (head_dim ** (-0.5)) * math.log2(math.e)

    me = lax.axis_index("ctx")
    z0 = lax.axis_index("tp")
    c0 = lax.rem(me, CORES)
    y0 = lax.rem(lax.div(me, CORES), ny)
    x0 = lax.div(me, CORES * ny)

    def at(x, y, c):
        return {"ctx": (x * ny + y) * CORES + c}

    def x_peer(d):
        return at(lax.rem(x0 + d + nx, nx), y0, c0)

    def y_peer(d):
        return at(x0, lax.rem(y0 + d + ny, ny), c0)

    sibling = at(x0, y0, 1 - c0)
    z_same = lax.axis_index("ctx")
    z_cross = (x0 * ny + y0) * CORES + 1 - c0

    def remote(src, dst, send, recv, device):
        return pltpu.make_async_remote_copy(
            src_ref=src,
            dst_ref=dst,
            send_sem=send,
            recv_sem=recv,
            device_id=device,
            device_id_type=MESH,
        )

    def family(number):
        return send_sem.at[number], recv_sem.at[number]

    def q_x(d):
        return remote(q_ref, qbuf.at[0, d], *family(0), x_peer(d))

    def q_y(d):
        return remote(qbuf.at[0], qbuf.at[d], send_sem.at[1], qy_sem.at[d], y_peer(d))

    def k_core():
        return remote(k_ref, kbuf.at[1], *family(2), sibling)

    def v_core():
        return remote(v_ref, vbuf.at[1, :, 0:head_dim], *family(3), sibling)

    def w_core():
        return remote(w_ref, wbuf.at[1], *family(4), sibling)

    def p_y(d):
        return remote(parts.at[d], y_parts.at[d], *family(5), y_peer(-d))

    def pt_y(d):
        return remote(part_tops.at[d], y_tops.at[d], *family(6), y_peer(-d))

    def p_x(d):
        return remote(merged.at[d], x_parts.at[d], *family(7), x_peer(-d))

    def pt_x(d):
        return remote(merged_top, x_tops.at[d], *family(8), x_peer(-d))

    def a_y(d):
        return remote(abuf.at[0, 0], abuf.at[0, d], *family(9), y_peer(d))

    def a_x(d):
        return remote(abuf.at[0], abuf.at[d], send_sem.at[10], recv_sem.at[11 + d], x_peer(d))

    def z_copy(dx, j, cross):
        z = lax.rem(x0 - dx + nx, nx) * (nz // nx) + j
        return z, remote(
            z_send.at[dx, j, cross],
            z_parts.at[z0 * CORES + c0],
            *family(11),
            {"ctx": z_cross if cross else z_same, "tp": z},
        )

    barrier = pltpu.get_barrier_semaphore()
    order = sorted(range(1, ny), key=lambda d: -min(d, ny - d))
    partners = [y_peer(d) for d in order] + [x_peer(d) for d in range(1, nx)] + [sibling]
    for d in sorted(range(1, nz), key=lambda d: -min(d, nz - d)):
        z = lax.rem(z0 + d, nz)
        partners += [{"ctx": z_same, "tp": z}, {"ctx": z_cross, "tp": z}]
    for partner in partners:
        pl.semaphore_signal(barrier, inc=1, device_id=partner, device_id_type=MESH)

    local = [
        pltpu.make_async_copy(q_ref, qbuf.at[0, 0], local_sem.at[0]),
        pltpu.make_async_copy(sk_ref, skbuf, local_sem.at[1]),
        pltpu.make_async_copy(nk_ref, nkbuf, local_sem.at[2]),
        pltpu.make_async_copy(nv_ref, nvbuf, local_sem.at[3]),
        pltpu.make_async_copy(sv_ref, svbuf, local_sem.at[4]),
        pltpu.make_async_copy(k_ref, kbuf.at[0], local_sem.at[5]),
        pltpu.make_async_copy(v_ref, vbuf.at[0, :, 0:head_dim], local_sem.at[6]),
        pltpu.make_async_copy(w_ref, wbuf.at[0], local_sem.at[7]),
    ]
    for copy in local:
        copy.start()
    for c in range(CORES):
        vbuf[c, :, head_dim:] = jnp.ones((keys, LANES), jnp.bfloat16)

    pl.semaphore_wait(barrier, len(partners))
    for d in range(1, nx):
        q_x(d).start()
    k_core().start()
    v_core().start()

    for copy in local[:5]:
        copy.wait()
    own_queries = qbuf[0, 0]
    row_in_sample = lax.broadcasted_iota(jnp.int32, (samp_rows, 1), 0)
    slot_index = lax.broadcasted_iota(jnp.int32, (samp_rows, slots), 1)
    tops = []
    for s in range(samp_dev):
        queries = own_queries[s * samp_rows : (s + 1) * samp_rows]
        scores = dot_rows(queries, skbuf[s])
        scores = jnp.where(slot_index < len_ref[s], scores, masked_score)
        new_keys = nkbuf[s].astype(jnp.float32)
        new_values = nvbuf[s].astype(jnp.float32)
        row_top = jnp.max(scores, axis=1, keepdims=True)
        recent = []
        for u in range(steps):
            score = jnp.sum(
                queries.astype(jnp.float32) * new_keys[u : u + 1], axis=1, keepdims=True
            )
            score = jnp.where(row_in_sample >= u * heads, score, masked_score)
            row_top = jnp.maximum(row_top, score)
            recent.append(score)
        weights = jnp.exp2((scores - row_top) * log2_scale)
        row_total = jnp.sum(weights, axis=1, keepdims=True)
        weighted = dot(weights.astype(jnp.bfloat16), svbuf[s])
        for u in range(steps):
            weight = jnp.exp2((recent[u] - row_top) * log2_scale)
            row_total = row_total + weight
            weighted = weighted + weight.astype(jnp.bfloat16).astype(jnp.float32) * (
                new_values[u : u + 1]
            )
        suffix_part[s * samp_rows : (s + 1) * samp_rows, :] = weighted / row_total
        tops.append(row_top * log2_scale + jnp.log2(row_total))
    lane = lax.broadcasted_iota(jnp.int32, (rows, LANES), 1)
    sub = lax.broadcasted_iota(jnp.int32, (rows, LANES), 0)
    suffix_top[...] = jnp.sum(
        jnp.where(lax.rem(lane, rows) == sub, jnp.concatenate(tops, axis=0), 0.0),
        axis=0,
        keepdims=True,
    )

    remote(qbuf.at[0, 1:nx], qbuf.at[0, 1:nx], *family(0), sibling).wait_recv()
    for d in range(1, ny):
        q_y(d).start()
    local[5].wait()
    local[6].wait()
    k_core().wait_recv()
    v_core().wait_recv()
    w_core().start()

    eye = lax.broadcasted_iota(jnp.int32, (LANES, LANES), 0) == lax.broadcasted_iota(
        jnp.int32, (LANES, LANES), 1
    )
    width = min(keys, 256)

    def attend(queries):
        row_top = weighted = None
        for c in range(CORES):
            for start in range(0, keys, width):
                scores = dot_rows(queries, kbuf[c, start : start + width])
                block_top = jnp.max(scores, axis=1, keepdims=True)
                top = block_top if row_top is None else jnp.maximum(row_top, block_top)
                weights = jnp.exp2((scores - top) * log2_scale).astype(jnp.bfloat16)
                term = dot(weights, vbuf[c, start : start + width])
                if row_top is not None:
                    term = weighted * jnp.exp2((row_top - top) * log2_scale) + term
                row_top, weighted = top, term
        total = weighted[:, head_dim:]
        part = (weighted[:, :head_dim] / total).astype(jnp.bfloat16)
        return part, row_top * log2_scale + jnp.log2(total)

    def pair(k, carry):
        first, second = 2 * k + 1, lax.rem(2 * k + 2, ny)
        q_y(first).wait_recv()

        @pl.when(second != 0)
        def _():
            q_y(second).wait_recv()

        queries = jnp.concatenate(
            [qbuf[first].reshape(line, head_dim), qbuf[second].reshape(line, head_dim)], axis=0
        )
        part, top = attend(queries)
        for i, slot in enumerate((first, second)):
            parts[slot] = part[i * line : (i + 1) * line].reshape(nx, rows, head_dim)
            part_tops[slot] = jnp.sum(
                jnp.where(eye, top[i * line : (i + 1) * line], 0.0), axis=0, keepdims=True
            )
        p_y(first).start()
        pt_y(first).start()

        @pl.when(second != 0)
        def _():
            p_y(second).start()
            pt_y(second).start()

        return carry

    lax.fori_loop(0, ny // 2, pair, 0)

    y_parts[0] = parts[0]
    y_tops[0] = part_tops[0]
    remote(parts.at[1:ny], y_parts.at[1:ny], *family(5), sibling).wait_recv()
    remote(part_tops.at[1:ny], y_tops.at[1:ny], *family(6), sibling).wait_recv()
    stats = [y_tops[d] for d in range(ny)]
    row_top = functools.reduce(jnp.maximum, stats)
    stats = [jnp.exp2(stat - row_top) for stat in stats]
    total = functools.reduce(jnp.add, stats)
    inverse = 1.0 / total
    result = jnp.zeros((line, head_dim), jnp.float32)
    for d in range(ny):
        spread = jnp.where(eye, stats[d] * inverse, 0.0).astype(jnp.bfloat16)
        result = result + dot(spread, y_parts[d].reshape(line, head_dim))
    merged[...] = result.astype(jnp.bfloat16).reshape(nx, rows, head_dim)
    merged_top[...] = row_top + jnp.log2(total)
    for d in range(1, nx):
        p_x(d).start()
        pt_x(d).start()
    x_parts[0] = merged[0]
    x_tops[0] = merged_top[...]
    remote(merged.at[1:nx], x_parts.at[1:nx], *family(7), sibling).wait_recv()
    remote(x_tops.at[1:nx], x_tops.at[1:nx], *family(8), sibling).wait_recv()

    lane_row = lax.broadcasted_iota(jnp.int32, (1, LANES), 1)
    flat = x_tops[0]
    for d in range(1, nx):
        flat = jnp.where(lax.div(lane_row, rows) == d, x_tops[d], flat)

    def over_groups(result, op):
        turn = LANES // 2
        while turn >= rows:
            result = op(result, pltpu.roll(result, turn, 1))
            turn //= 2
        return result

    own_top = suffix_top[...]
    row_top = jnp.maximum(over_groups(flat, jnp.maximum), own_top)
    flat = jnp.exp2(flat - row_top)
    own_weight = jnp.exp2(own_top - row_top)
    inverse = 1.0 / (over_groups(flat, jnp.add) + own_weight)
    own_column = jnp.sum(
        jnp.where(lane == sub, own_weight * inverse, 0.0), axis=1, keepdims=True
    )
    spread = jnp.where(lax.rem(lane, rows) == sub, flat * inverse, 0.0).astype(jnp.bfloat16)
    result = own_column * suffix_part[...] + dot(spread, x_parts[...].reshape(line, head_dim))
    abuf[0, 0] = result.astype(jnp.bfloat16)

    for d in order:
        a_y(d).start()
    w_core().wait_recv()
    local[7].wait()
    remote(abuf.at[0, 1:ny], abuf.at[0, 1:ny], *family(9), sibling).wait_recv()
    for d in range(1, nx):
        a_x(d).start()

    share = ny * tokens * nx // nz

    def project(dx):
        for d in range(ny):
            place = pl.multiple_of(lax.rem(y0 - d + ny, ny) * rows, rows)
            attention32[dx, pl.ds(place, rows), :] = abuf[dx, d].astype(jnp.float32)
        features = jnp.concatenate(
            [
                attention32[dx, pl.ds(h, ny * tokens, stride=heads), :].astype(jnp.bfloat16)
                for h in range(heads)
            ],
            axis=1,
        )
        for cross in range(CORES):
            terms = dot(features, wbuf[cross]).astype(jnp.bfloat16)
            for j in range(nz // nx):
                z_send[dx, j, cross] = terms[j * share : (j + 1) * share]
        for j in range(nz // nx):
            z, copy = z_copy(dx, j, 0)
            z_copy(dx, j, 1)[1].start()

            @pl.when(z != z0)
            def _():
                copy.start()

            @pl.when(z == z0)
            def _():
                z_parts[z0 * CORES + c0] = z_send[dx, j, 0]

    project(0)
    for dx in sorted(range(1, nx), key=lambda d: min(d, nx - d)):
        a_x(dx).wait_recv()
        project(dx)

    sources = nz * CORES
    remote(z_parts.at[1:sources], z_parts.at[1:sources], *family(11), sibling).wait_recv()
    total = []
    for c in range(CORES):
        terms = z_parts[c].astype(jnp.float32)
        for z in range(1, nz):
            terms = terms + z_parts[z * CORES + c].astype(jnp.float32)
        total.append(terms.astype(jnp.bfloat16))
    row_out = lax.broadcasted_iota(jnp.int32, (CORES * share, CORES * share), 0)
    row_in = lax.broadcasted_iota(jnp.int32, (CORES * share, CORES * share), 1)
    core = lax.rem(lax.div(row_out, tokens), CORES)
    source = (
        core * share + lax.div(row_out, CORES * tokens) * tokens + lax.rem(row_out, tokens)
    )
    reorder = jnp.where(row_in == source, 1.0, 0.0).astype(jnp.bfloat16)
    out_ref[...] = dot(reorder, jnp.concatenate(total, axis=0)).astype(jnp.bfloat16)

    remote(qbuf.at[0, 1:nx], qbuf.at[0, 1:nx], *family(0), sibling).wait_send()
    remote(qbuf.at[1:ny], qbuf.at[1:ny], send_sem.at[1], qy_sem.at[1], sibling).wait_send()
    for copy in (k_core, v_core, w_core):
        copy().wait_send()
    remote(parts.at[1:ny], y_parts.at[1:ny], *family(5), sibling).wait_send()
    remote(part_tops.at[1:ny], y_tops.at[1:ny], *family(6), sibling).wait_send()
    remote(merged.at[1:nx], x_parts.at[1:nx], *family(7), sibling).wait_send()
    remote(x_tops.at[1:nx], x_tops.at[1:nx], *family(8), sibling).wait_send()
    remote(abuf.at[0, 1:ny], abuf.at[0, 1:ny], *family(9), sibling).wait_send()
    remote(abuf.at[1:nx], abuf.at[1:nx], send_sem.at[10], recv_sem.at[10], sibling).wait_send()
    remote(z_parts.at[1:sources], z_parts.at[1:sources], *family(11), sibling).wait_send()


def per_device(
    sizes,
    queries,
    prefix_keys,
    prefix_values,
    suffix_keys,
    suffix_values,
    new_keys,
    new_values,
    suffix_lengths,
    out_weight,
):
    nx, ny, nz = sizes
    samp_dev, steps, heads, head_dim = queries.shape
    rows = samp_dev * steps * heads
    tokens = samp_dev * steps
    keys = prefix_keys.shape[0]
    slots = suffix_keys.shape[1]
    columns = out_weight.shape[1]
    share = ny * tokens * nx // nz
    bf16, f32 = jnp.bfloat16, jnp.float32
    anywhere = pl.BlockSpec(memory_space=pl.ANY)
    out = pl.pallas_call(
        functools.partial(attend_kernel, sizes),
        out_shape=jax.ShapeDtypeStruct((CORES * share, columns), bf16),
        in_specs=[anywhere] * 7 + [pl.BlockSpec(memory_space=pltpu.SMEM), anywhere],
        out_specs=pl.BlockSpec(memory_space=pltpu.VMEM),
        scratch_shapes=[
            pltpu.VMEM((CORES, keys, head_dim), bf16),
            pltpu.VMEM((CORES, keys, head_dim + LANES), bf16),
            pltpu.VMEM((samp_dev, slots, head_dim), bf16),
            pltpu.VMEM((samp_dev, slots, head_dim), bf16),
            pltpu.VMEM((samp_dev, steps, head_dim), bf16),
            pltpu.VMEM((samp_dev, steps, head_dim), bf16),
            pltpu.VMEM((CORES, heads * head_dim, columns), bf16),
            pltpu.VMEM((ny, nx, rows, head_dim), bf16),
            pltpu.VMEM((ny, nx, rows, head_dim), bf16),
            pltpu.VMEM((ny, 1, LANES), f32),
            pltpu.VMEM((ny, nx, rows, head_dim), bf16),
            pltpu.VMEM((ny, 1, LANES), f32),
            pltpu.VMEM((nx, rows, head_dim), bf16),
            pltpu.VMEM((1, LANES), f32),
            pltpu.VMEM((nx, rows, head_dim), bf16),
            pltpu.VMEM((nx, 1, LANES), f32),
            pltpu.VMEM((rows, head_dim), f32),
            pltpu.VMEM((1, LANES), f32),
            pltpu.VMEM((nx, ny, rows, head_dim), bf16),
            pltpu.VMEM((nx, ny * rows, head_dim), f32),
            pltpu.VMEM((nx, nz // nx, CORES, share, columns), bf16),
            pltpu.VMEM((nz * CORES, share, columns), bf16),
            pltpu.SemaphoreType.DMA((8,)),
            pltpu.SemaphoreType.DMA((12,)),
            pltpu.SemaphoreType.DMA((11 + nx,)),
            pltpu.SemaphoreType.DMA((ny,)),
        ],
        compiler_params=pltpu.CompilerParams(
            collective_id=0, has_side_effects=True, vmem_limit_bytes=60 * 1024 * 1024
        ),
    )(
        queries.reshape(rows, head_dim),
        prefix_keys.reshape(keys, head_dim),
        prefix_values.reshape(keys, head_dim),
        suffix_keys.reshape(samp_dev, slots, head_dim),
        suffix_values.reshape(samp_dev, slots, head_dim),
        new_keys.reshape(samp_dev, steps, head_dim),
        new_values.reshape(samp_dev, steps, head_dim),
        suffix_lengths,
        out_weight,
    )
    return out.reshape(CORES * share // steps, steps, columns)


def solution(mesh, sizes=(4, 8, 8)):
    placed = (
        P("ctx", None, "tp", None),
        P("ctx", "tp", None),
        P("ctx", "tp", None),
        P("ctx", None, "tp", None),
        P("ctx", None, "tp", None),
        P("ctx", None, "tp", None),
        P("ctx", None, "tp", None),
        P("ctx"),
        P("tp", "ctx"),
    )
    return jax.shard_map(
        functools.partial(per_device, sizes),
        mesh=mesh,
        in_specs=placed,
        out_specs=P("tp", None, "ctx"),
        check_vma=False,
    )
```

time: 64.9 us -> 54.5 us (0.84)
  the two profiles are of different devices: /device:TPU:3 before, /device:TPU:4 now
where the time goes in v2:
time: 54.5 us; the launch traced here: 54.3 us
  Pallas kernels  53 us (97%)
  local copies, waits for them, and re-layouts  1.3 us (2%)
    pallas_call x1, Pallas kernels, per_device(): pl.pallas_call(functools.partial(attend_kernel, sizes), out_shape=jax.Sha...  53 us
    unnamed x1, local copies, waits for them, and re-layouts  1.3 us

profile of v2, /device:TPU:4, one launch (start us, length us, event | category | flops | bytes accessed | tf_op | source)
XLA Modules:
  0.0 54.3 jit_solution(16752285774622210108)
XLA Ops:
  0.0 53.0 %shard_map.91 = bf16[32,128]{1,0:T(8,128)(2,1)} custom-call(bf16[32,128]{1,0:T(8,128)(2,1)} %bitcast.13, bf16[2048,128]{1,0:T(8,128)(2,1)} %bitcast.8, bf16[2048,128]{1,0:T(8,128)(2,1)} %bitcast.9, bf16[2,1024,128]{2,1,0:T(8,128)(2,1)} %bitcast.10, bf16[2,1024,128]{2,1,0:T(8,128)(2,1)} %bitcast.11, bf16[2,2,128]{2,1,0:T(2,128)(2,1)} %bitcast.14, ...), custom_call_target="tpu_custom_call" | custom-call | tf_op jit(solution)/shard_map/pallas_call | solution.py:421
  53.0 1.3 %copy.11 = bf16[16,2,128]{2,1,0:T(2,128)(2,1)} copy(bf16[16,2,128]{2,1,0:T(2,128)(2,1)} %bitcast.12) | data formatting | bytes 16384

commit v3 on v2

--- a/solution.py
+++ b/solution.py
@@ -46,12 +46,8 @@
     qbuf,
     parts,
     part_tops,
-    y_parts,
-    y_tops,
-    merged,
-    merged_top,
-    x_parts,
-    x_tops,
+    got,
+    got_tops,
     suffix_part,
     suffix_top,
     abuf,
@@ -61,7 +57,7 @@
     local_sem,
     send_sem,
     recv_sem,
-    qy_sem,
+    q_sem,
 ):
     nx, ny, nz = sizes
     rows, head_dim = q_ref.shape
@@ -83,11 +79,14 @@
     def at(x, y, c):
         return {"ctx": (x * ny + y) * CORES + c}
 
+    def peer(dx, dy):
+        return at(lax.rem(x0 + dx + nx, nx), lax.rem(y0 + dy + ny, ny), c0)
+
     def x_peer(d):
-        return at(lax.rem(x0 + d + nx, nx), y0, c0)
+        return peer(d, 0)
 
     def y_peer(d):
-        return at(x0, lax.rem(y0 + d + ny, ny), c0)
+        return peer(0, d)
 
     sibling = at(x0, y0, 1 - c0)
     z_same = lax.axis_index("ctx")
@@ -106,11 +105,10 @@
     def family(number):
         return send_sem.at[number], recv_sem.at[number]
 
-    def q_x(d):
-        return remote(q_ref, qbuf.at[0, d], *family(0), x_peer(d))
-
-    def q_y(d):
-        return remote(qbuf.at[0], qbuf.at[d], send_sem.at[1], qy_sem.at[d], y_peer(d))
+    def q_copy(dx, dy):
+        return remote(
+            qbuf.at[0, 0], qbuf.at[dy, dx], send_sem.at[0], q_sem.at[dy], peer(dx, dy)
+        )
 
     def k_core():
         return remote(k_ref, kbuf.at[1], *family(2), sibling)
@@ -121,17 +119,17 @@
     def w_core():
         return remote(w_ref, wbuf.at[1], *family(4), sibling)
 
-    def p_y(d):
-        return remote(parts.at[d], y_parts.at[d], *family(5), y_peer(-d))
-
-    def pt_y(d):
-        return remote(part_tops.at[d], y_tops.at[d], *family(6), y_peer(-d))
-
-    def p_x(d):
-        return remote(merged.at[d], x_parts.at[d], *family(7), x_peer(-d))
-
-    def pt_x(d):
-        return remote(merged_top, x_tops.at[d], *family(8), x_peer(-d))
+    def p_copy(dx, dy):
+        return remote(parts.at[dy, dx], got.at[dy, dx], *family(5), peer(-dx, -dy))
+
+    def pt_copy(dx, dy):
+        return remote(part_tops.at[dy], got_tops.at[dy, dx], *family(6), peer(-dx, -dy))
+
+    def own_line_copy(dx):
+        return (
+            remote(parts.at[0, dx], got.at[0, dx], *family(7), peer(-dx, 0)),
+            remote(part_tops.at[0], got_tops.at[0, dx], *family(8), peer(-dx, 0)),
+        )
 
     def a_y(d):
         return remote(abuf.at[0, 0], abuf.at[0, d], *family(9), y_peer(d))
@@ -150,7 +148,9 @@
 
     barrier = pltpu.get_barrier_semaphore()
     order = sorted(range(1, ny), key=lambda d: -min(d, ny - d))
-    partners = [y_peer(d) for d in order] + [x_peer(d) for d in range(1, nx)] + [sibling]
+    others = [(dx, dy) for dy in [*range(1, ny), 0] for dx in range(nx) if dx or dy]
+    others.sort(key=lambda d: -min(d[0], nx - d[0]) - min(d[1], ny - d[1]))
+    partners = [peer(dx, dy) for dx, dy in others] + [sibling]
     for d in sorted(range(1, nz), key=lambda d: -min(d, nz - d)):
         z = lax.rem(z0 + d, nz)
         partners += [{"ctx": z_same, "tp": z}, {"ctx": z_cross, "tp": z}]
@@ -173,12 +173,15 @@
         vbuf[c, :, head_dim:] = jnp.ones((keys, LANES), jnp.bfloat16)
 
     pl.semaphore_wait(barrier, len(partners))
-    for d in range(1, nx):
-        q_x(d).start()
+    local[0].wait()
+    for dy in [*range(1, ny), 0]:
+        for dx in range(nx):
+            if dx or dy:
+                q_copy(dx, dy).start()
     k_core().start()
     v_core().start()
 
-    for copy in local[:5]:
+    for copy in local[1:5]:
         copy.wait()
     own_queries = qbuf[0, 0]
     row_in_sample = lax.broadcasted_iota(jnp.int32, (samp_rows, 1), 0)
@@ -218,9 +221,6 @@
         keepdims=True,
     )
 
-    remote(qbuf.at[0, 1:nx], qbuf.at[0, 1:nx], *family(0), sibling).wait_recv()
-    for d in range(1, ny):
-        q_y(d).start()
     local[5].wait()
     local[6].wait()
     k_core().wait_recv()
@@ -248,13 +248,21 @@
         part = (weighted[:, :head_dim] / total).astype(jnp.bfloat16)
         return part, row_top * log2_scale + jnp.log2(total)
 
+    def line_arrived(dy):
+        return remote(qbuf.at[dy], qbuf.at[dy], send_sem.at[0], q_sem.at[dy], sibling)
+
     def pair(k, carry):
         first, second = 2 * k + 1, lax.rem(2 * k + 2, ny)
-        q_y(first).wait_recv()
+        line_arrived(first).wait_recv()
 
         @pl.when(second != 0)
         def _():
-            q_y(second).wait_recv()
+            line_arrived(second).wait_recv()
+
+        @pl.when(second == 0)
+        def _():
+            mine = qbuf.at[0, 1:nx]
+            remote(mine, mine, send_sem.at[0], q_sem.at[0], sibling).wait_recv()
 
         queries = jnp.concatenate(
             [qbuf[first].reshape(line, head_dim), qbuf[second].reshape(line, head_dim)], axis=0
@@ -265,45 +273,41 @@
             part_tops[slot] = jnp.sum(
                 jnp.where(eye, top[i * line : (i + 1) * line], 0.0), axis=0, keepdims=True
             )
-        p_y(first).start()
-        pt_y(first).start()
+        for dx in range(nx):
+            p_copy(dx, first).start()
+            pt_copy(dx, first).start()
 
         @pl.when(second != 0)
         def _():
-            p_y(second).start()
-            pt_y(second).start()
+            for dx in range(nx):
+                p_copy(dx, second).start()
+                pt_copy(dx, second).start()
 
         return carry
 
     lax.fori_loop(0, ny // 2, pair, 0)
 
-    y_parts[0] = parts[0]
-    y_tops[0] = part_tops[0]
-    remote(parts.at[1:ny], y_parts.at[1:ny], *family(5), sibling).wait_recv()
-    remote(part_tops.at[1:ny], y_tops.at[1:ny], *family(6), sibling).wait_recv()
-    stats = [y_tops[d] for d in range(ny)]
-    row_top = functools.reduce(jnp.maximum, stats)
-    stats = [jnp.exp2(stat - row_top) for stat in stats]
-    total = functools.reduce(jnp.add, stats)
-    inverse = 1.0 / total
-    result = jnp.zeros((line, head_dim), jnp.float32)
-    for d in range(ny):
-        spread = jnp.where(eye, stats[d] * inverse, 0.0).astype(jnp.bfloat16)
-        result = result + dot(spread, y_parts[d].reshape(line, head_dim))
-    merged[...] = result.astype(jnp.bfloat16).reshape(nx, rows, head_dim)
-    merged_top[...] = row_top + jnp.log2(total)
-    for d in range(1, nx):
-        p_x(d).start()
-        pt_x(d).start()
-    x_parts[0] = merged[0]
-    x_tops[0] = merged_top[...]
-    remote(merged.at[1:nx], x_parts.at[1:nx], *family(7), sibling).wait_recv()
-    remote(x_tops.at[1:nx], x_tops.at[1:nx], *family(8), sibling).wait_recv()
+    for dx in range(1, nx):
+        for copy in own_line_copy(dx):
+            copy.start()
+    got[0, 0] = parts[0, 0]
+    got_tops[0, 0] = part_tops[0]
+    arrivals = (
+        (got.at[1:ny], *family(5)),
+        (got_tops.at[1:ny], *family(6)),
+        (got.at[0, 1:nx], *family(7)),
+        (got_tops.at[0, 1:nx], *family(8)),
+    )
+    for ref, send, recv in arrivals:
+        remote(ref, ref, send, recv, sibling).wait_recv()
 
     lane_row = lax.broadcasted_iota(jnp.int32, (1, LANES), 1)
-    flat = x_tops[0]
-    for d in range(1, nx):
-        flat = jnp.where(lax.div(lane_row, rows) == d, x_tops[d], flat)
+    stats = []
+    for dy in range(ny):
+        flat = got_tops[dy, 0]
+        for dx in range(1, nx):
+            flat = jnp.where(lax.div(lane_row, rows) == dx, got_tops[dy, dx], flat)
+        stats.append(flat)
 
     def over_groups(result, op):
         turn = LANES // 2
@@ -313,15 +317,19 @@
         return result
 
     own_top = suffix_top[...]
-    row_top = jnp.maximum(over_groups(flat, jnp.maximum), own_top)
-    flat = jnp.exp2(flat - row_top)
+    row_top = jnp.maximum(
+        over_groups(functools.reduce(jnp.maximum, stats), jnp.maximum), own_top
+    )
+    stats = [jnp.exp2(flat - row_top) for flat in stats]
     own_weight = jnp.exp2(own_top - row_top)
-    inverse = 1.0 / (over_groups(flat, jnp.add) + own_weight)
+    inverse = 1.0 / (over_groups(functools.reduce(jnp.add, stats), jnp.add) + own_weight)
     own_column = jnp.sum(
         jnp.where(lane == sub, own_weight * inverse, 0.0), axis=1, keepdims=True
     )
-    spread = jnp.where(lax.rem(lane, rows) == sub, flat * inverse, 0.0).astype(jnp.bfloat16)
-    result = own_column * suffix_part[...] + dot(spread, x_parts[...].reshape(line, head_dim))
+    result = own_column * suffix_part[...]
+    for dy in range(ny):
+        spread = jnp.where(lax.rem(lane, rows) == sub, stats[dy] * inverse, 0.0)
+        result = result + dot(spread.astype(jnp.bfloat16), got[dy].reshape(line, head_dim))
     abuf[0, 0] = result.astype(jnp.bfloat16)
 
     for d in order:
@@ -383,14 +391,14 @@
     reorder = jnp.where(row_in == source, 1.0, 0.0).astype(jnp.bfloat16)
     out_ref[...] = dot(reorder, jnp.concatenate(total, axis=0)).astype(jnp.bfloat16)
 
-    remote(qbuf.at[0, 1:nx], qbuf.at[0, 1:nx], *family(0), sibling).wait_send()
-    remote(qbuf.at[1:ny], qbuf.at[1:ny], send_sem.at[1], qy_sem.at[1], sibling).wait_send()
+    sent = qbuf.at[1:ny]
+    remote(sent, sent, send_sem.at[0], q_sem.at[1], sibling).wait_send()
+    sent = qbuf.at[0, 1:nx]
+    remote(sent, sent, send_sem.at[0], q_sem.at[0], sibling).wait_send()
     for copy in (k_core, v_core, w_core):
         copy().wait_send()
-    remote(parts.at[1:ny], y_parts.at[1:ny], *family(5), sibling).wait_send()
-    remote(part_tops.at[1:ny], y_tops.at[1:ny], *family(6), sibling).wait_send()
-    remote(merged.at[1:nx], x_parts.at[1:nx], *family(7), sibling).wait_send()
-    remote(x_tops.at[1:nx], x_tops.at[1:nx], *family(8), sibling).wait_send()
+    for ref, send, recv in arrivals:
+        remote(ref, ref, send, recv, sibling).wait_send()
     remote(abuf.at[0, 1:ny], abuf.at[0, 1:ny], *family(9), sibling).wait_send()
     remote(abuf.at[1:nx], abuf.at[1:nx], send_sem.at[10], recv_sem.at[10], sibling).wait_send()
     remote(z_parts.at[1:sources], z_parts.at[1:sources], *family(11), sibling).wait_send()
@@ -435,11 +443,7 @@
             pltpu.VMEM((ny, nx, rows, head_dim), bf16),
             pltpu.VMEM((ny, 1, LANES), f32),
             pltpu.VMEM((ny, nx, rows, head_dim), bf16),
-            pltpu.VMEM((ny, 1, LANES), f32),
-            pltpu.VMEM((nx, rows, head_dim), bf16),
-            pltpu.VMEM((1, LANES), f32),
-            pltpu.VMEM((nx, rows, head_dim), bf16),
-            pltpu.VMEM((nx, 1, LANES), f32),
+            pltpu.VMEM((ny, nx, 1, LANES), f32),
             pltpu.VMEM((rows, head_dim), f32),
             pltpu.VMEM((1, LANES), f32),
             pltpu.VMEM((nx, ny, rows, head_dim), bf16),

time: 54.5 us -> 51.3 us (0.941)
  the two profiles are of different devices: /device:TPU:4 before, /device:TPU:5 now
where the time goes in v3:
time: 51.3 us; the launch traced here: 51.1 us
  Pallas kernels  49.8 us (97%)
  local copies, waits for them, and re-layouts  1.3 us (3%)
    pallas_call x1, Pallas kernels, per_device(): pl.pallas_call(functools.partial(attend_kernel, sizes), out_shape=jax.Sha...  49.8 us
    unnamed x1, local copies, waits for them, and re-layouts  1.3 us

profile of v3, /device:TPU:5, one launch (start us, length us, event | category | flops | bytes accessed | tf_op | source)
XLA Modules:
  0.0 51.1 jit_solution(13885489671374382353)
XLA Ops:
  0.0 49.8 %shard_map.91 = bf16[32,128]{1,0:T(8,128)(2,1)} custom-call(bf16[32,128]{1,0:T(8,128)(2,1)} %bitcast.13, bf16[2048,128]{1,0:T(8,128)(2,1)} %bitcast.8, bf16[2048,128]{1,0:T(8,128)(2,1)} %bitcast.9, bf16[2,1024,128]{2,1,0:T(8,128)(2,1)} %bitcast.10, bf16[2,1024,128]{2,1,0:T(8,128)(2,1)} %bitcast.11, bf16[2,2,128]{2,1,0:T(2,128)(2,1)} %bitcast.14, ...), custom_call_target="tpu_custom_call" | custom-call | tf_op jit(solution)/shard_map/pallas_call | solution.py:429
  49.8 1.3 %copy.11 = bf16[16,2,128]{2,1,0:T(2,128)(2,1)} copy(bf16[16,2,128]{2,1,0:T(2,128)(2,1)} %bitcast.12) | data formatting | bytes 16384

commit v4 on v3

--- a/solution.py
+++ b/solution.py
@@ -58,6 +58,7 @@
     send_sem,
     recv_sem,
     q_sem,
+    a_sem,
 ):
     nx, ny, nz = sizes
     rows, head_dim = q_ref.shape
@@ -89,6 +90,7 @@
         return peer(0, d)
 
     sibling = at(x0, y0, 1 - c0)
+    far_first = sorted(range(nx), key=lambda d: -min(d, nx - d))
     z_same = lax.axis_index("ctx")
     z_cross = (x0 * ny + y0) * CORES + 1 - c0
 
@@ -132,10 +134,12 @@
         )
 
     def a_y(d):
-        return remote(abuf.at[0, 0], abuf.at[0, d], *family(9), y_peer(d))
-
-    def a_x(d):
-        return remote(abuf.at[0], abuf.at[d], send_sem.at[10], recv_sem.at[11 + d], x_peer(d))
+        return remote(abuf.at[0, 0], abuf.at[0, d], send_sem.at[9], a_sem.at[d], y_peer(d))
+
+    def a_x(d, dy):
+        return remote(
+            abuf.at[0, dy], abuf.at[d, dy], send_sem.at[10], recv_sem.at[11 + d], x_peer(d)
+        )
 
     def z_copy(dx, j, cross):
         z = lax.rem(x0 - dx + nx, nx) * (nz // nx) + j
@@ -174,8 +178,12 @@
 
     pl.semaphore_wait(barrier, len(partners))
     local[0].wait()
-    for dy in [*range(1, ny), 0]:
-        for dx in range(nx):
+    lines = []
+    for k in range(ny // 2):
+        first = 1 + (k + 1) % (ny // 2)
+        lines += [first, (ny - first) * (1 - first // (ny // 2))]
+    for dy in lines:
+        for dx in far_first:
             if dx or dy:
                 q_copy(dx, dy).start()
     k_core().start()
@@ -251,8 +259,11 @@
     def line_arrived(dy):
         return remote(qbuf.at[dy], qbuf.at[dy], send_sem.at[0], q_sem.at[dy], sibling)
 
+    half = ny // 2
+
     def pair(k, carry):
-        first, second = 2 * k + 1, lax.rem(2 * k + 2, ny)
+        first = 1 + lax.rem(k + 1, half)
+        second = (ny - first) * (1 - lax.div(first, half))
         line_arrived(first).wait_recv()
 
         @pl.when(second != 0)
@@ -273,23 +284,27 @@
             part_tops[slot] = jnp.sum(
                 jnp.where(eye, top[i * line : (i + 1) * line], 0.0), axis=0, keepdims=True
             )
-        for dx in range(nx):
+        for dx in far_first:
             p_copy(dx, first).start()
             pt_copy(dx, first).start()
 
         @pl.when(second != 0)
         def _():
-            for dx in range(nx):
+            for dx in far_first:
                 p_copy(dx, second).start()
                 pt_copy(dx, second).start()
 
+        @pl.when(second == 0)
+        def _():
+            for dx in far_first:
+                if dx:
+                    for copy in own_line_copy(dx):
+                        copy.start()
+
         return carry
 
     lax.fori_loop(0, ny // 2, pair, 0)
 
-    for dx in range(1, nx):
-        for copy in own_line_copy(dx):
-            copy.start()
     got[0, 0] = parts[0, 0]
     got_tops[0, 0] = part_tops[0]
     arrivals = (
@@ -334,11 +349,16 @@
 
     for d in order:
         a_y(d).start()
+    for d in far_first:
+        if d:
+            a_x(d, 0).start()
     w_core().wait_recv()
     local[7].wait()
-    remote(abuf.at[0, 1:ny], abuf.at[0, 1:ny], *family(9), sibling).wait_recv()
-    for d in range(1, nx):
-        a_x(d).start()
+    for dy in reversed(order):
+        a_y(dy).wait_recv()
+        for d in far_first:
+            if d:
+                a_x(d, dy).start()
 
     share = ny * tokens * nx // nz
 
@@ -371,7 +391,8 @@
 
     project(0)
     for dx in sorted(range(1, nx), key=lambda d: min(d, nx - d)):
-        a_x(dx).wait_recv()
+        came = abuf.at[dx]
+        remote(came, came, send_sem.at[10], recv_sem.at[11 + dx], sibling).wait_recv()
         project(dx)
 
     sources = nz * CORES
@@ -399,7 +420,7 @@
         copy().wait_send()
     for ref, send, recv in arrivals:
         remote(ref, ref, send, recv, sibling).wait_send()
-    remote(abuf.at[0, 1:ny], abuf.at[0, 1:ny], *family(9), sibling).wait_send()
+    remote(abuf.at[0, 1:ny], abuf.at[0, 1:ny], send_sem.at[9], a_sem.at[0], sibling).wait_send()
     remote(abuf.at[1:nx], abuf.at[1:nx], send_sem.at[10], recv_sem.at[10], sibling).wait_send()
     remote(z_parts.at[1:sources], z_parts.at[1:sources], *family(11), sibling).wait_send()
 
@@ -454,6 +475,7 @@
             pltpu.SemaphoreType.DMA((12,)),
             pltpu.SemaphoreType.DMA((11 + nx,)),
             pltpu.SemaphoreType.DMA((ny,)),
+            pltpu.SemaphoreType.DMA((ny,)),
         ],
         compiler_params=pltpu.CompilerParams(
             collective_id=0, has_side_effects=True, vmem_limit_bytes=60 * 1024 * 1024

time: 51.3 us -> 48.5 us (0.945)
  the two profiles are of different devices: /device:TPU:5 before, /device:TPU:3 now
where the time goes in v4:
time: 48.5 us; the launch traced here: 48.3 us
  Pallas kernels  47 us (97%)
  local copies, waits for them, and re-layouts  1.3 us (3%)
    pallas_call x1, Pallas kernels, per_device(): pl.pallas_call(functools.partial(attend_kernel, sizes), out_shape=jax.Sha...  47 us
    unnamed x1, local copies, waits for them, and re-layouts  1.3 us

profile of v4, /device:TPU:3, one launch (start us, length us, event | category | flops | bytes accessed | tf_op | source)
XLA Modules:
  0.0 48.3 jit_solution(16868377504207210411)
XLA Ops:
  0.0 47.0 %shard_map.91 = bf16[32,128]{1,0:T(8,128)(2,1)} custom-call(bf16[32,128]{1,0:T(8,128)(2,1)} %bitcast.13, bf16[2048,128]{1,0:T(8,128)(2,1)} %bitcast.8, bf16[2048,128]{1,0:T(8,128)(2,1)} %bitcast.9, bf16[2,1024,128]{2,1,0:T(8,128)(2,1)} %bitcast.10, bf16[2,1024,128]{2,1,0:T(8,128)(2,1)} %bitcast.11, bf16[2,2,128]{2,1,0:T(2,128)(2,1)} %bitcast.14, ...), custom_call_target="tpu_custom_call" | custom-call | tf_op jit(solution)/shard_map/pallas_call | solution.py:450
  47.0 1.3 %copy.11 = bf16[16,2,128]{2,1,0:T(2,128)(2,1)} copy(bf16[16,2,128]{2,1,0:T(2,128)(2,1)} %bitcast.12) | data formatting | bytes 16384

commit v5 on v4

--- a/solution.py
+++ b/solution.py
@@ -180,7 +180,7 @@
     local[0].wait()
     lines = []
     for k in range(ny // 2):
-        first = 1 + (k + 1) % (ny // 2)
+        first = 1 + (k + 2) % (ny // 2)
         lines += [first, (ny - first) * (1 - first // (ny // 2))]
     for dy in lines:
         for dx in far_first:
@@ -261,49 +261,54 @@
 
     half = ny // 2
 
-    def pair(k, carry):
-        first = 1 + lax.rem(k + 1, half)
-        second = (ny - first) * (1 - lax.div(first, half))
-        line_arrived(first).wait_recv()
-
-        @pl.when(second != 0)
-        def _():
-            line_arrived(second).wait_recv()
-
-        @pl.when(second == 0)
-        def _():
-            mine = qbuf.at[0, 1:nx]
-            remote(mine, mine, send_sem.at[0], q_sem.at[0], sibling).wait_recv()
-
+    def four(k, carry):
+        pairs = []
+        for i in range(2):
+            first = 1 + lax.rem(2 * k + i + 2, half)
+            pairs.append((first, (ny - first) * (1 - lax.div(first, half))))
+        for first, second in pairs:
+            line_arrived(first).wait_recv()
+
+            @pl.when(second != 0)
+            def _():
+                line_arrived(second).wait_recv()
+
+            @pl.when(second == 0)
+            def _():
+                mine = qbuf.at[0, 1:nx]
+                remote(mine, mine, send_sem.at[0], q_sem.at[0], sibling).wait_recv()
+
+        lines = [slot for both in pairs for slot in both]
         queries = jnp.concatenate(
-            [qbuf[first].reshape(line, head_dim), qbuf[second].reshape(line, head_dim)], axis=0
+            [qbuf[slot].reshape(line, head_dim) for slot in lines], axis=0
         )
         part, top = attend(queries)
-        for i, slot in enumerate((first, second)):
+        for i, slot in enumerate(lines):
             parts[slot] = part[i * line : (i + 1) * line].reshape(nx, rows, head_dim)
             part_tops[slot] = jnp.sum(
                 jnp.where(eye, top[i * line : (i + 1) * line], 0.0), axis=0, keepdims=True
             )
-        for dx in far_first:
-            p_copy(dx, first).start()
-            pt_copy(dx, first).start()
-
-        @pl.when(second != 0)
-        def _():
+        for first, second in pairs[::-1]:
             for dx in far_first:
-                p_copy(dx, second).start()
-                pt_copy(dx, second).start()
-
-        @pl.when(second == 0)
-        def _():
-            for dx in far_first:
-                if dx:
-                    for copy in own_line_copy(dx):
-                        copy.start()
+                p_copy(dx, first).start()
+                pt_copy(dx, first).start()
+
+            @pl.when(second != 0)
+            def _():
+                for dx in far_first:
+                    p_copy(dx, second).start()
+                    pt_copy(dx, second).start()
+
+            @pl.when(second == 0)
+            def _():
+                for dx in far_first:
+                    if dx:
+                        for copy in own_line_copy(dx):
+                            copy.start()
 
         return carry
 
-    lax.fori_loop(0, ny // 2, pair, 0)
+    lax.fori_loop(0, ny // 4, four, 0)
 
     got[0, 0] = parts[0, 0]
     got_tops[0, 0] = part_tops[0]

time: 48.5 us -> 50.2 us (1.035)
  Pallas kernels: 47 us -> 48.7 us
    pallas_call x1, Pallas kernels: 47 us -> 48.7 us  [per_device(): pl.pallas_call(functools.partial(attend_kernel, sizes), out_shape=jax.Sha...]
where the time goes in v5:
time: 50.2 us; the launch traced here: 50 us
  Pallas kernels  48.7 us (97%)
  local copies, waits for them, and re-layouts  1.3 us (3%)
    pallas_call x1, Pallas kernels, per_device(): pl.pallas_call(functools.partial(attend_kernel, sizes), out_shape=jax.Sha...  48.7 us
    unnamed x1, local copies, waits for them, and re-layouts  1.3 us

profile of v5, /device:TPU:3, one launch (start us, length us, event | category | flops | bytes accessed | tf_op | source)
XLA Modules:
  0.0 50.0 jit_solution(4747937613143073759)
XLA Ops:
  0.0 48.7 %shard_map.91 = bf16[32,128]{1,0:T(8,128)(2,1)} custom-call(bf16[32,128]{1,0:T(8,128)(2,1)} %bitcast.13, bf16[2048,128]{1,0:T(8,128)(2,1)} %bitcast.8, bf16[2048,128]{1,0:T(8,128)(2,1)} %bitcast.9, bf16[2,1024,128]{2,1,0:T(8,128)(2,1)} %bitcast.10, bf16[2,1024,128]{2,1,0:T(8,128)(2,1)} %bitcast.11, bf16[2,2,128]{2,1,0:T(2,128)(2,1)} %bitcast.14, ...), custom_call_target="tpu_custom_call" | custom-call | tf_op jit(solution)/shard_map/pallas_call | solution.py:455
  48.7 1.3 %copy.11 = bf16[16,2,128]{2,1,0:T(2,128)(2,1)} copy(bf16[16,2,128]{2,1,0:T(2,128)(2,1)} %bitcast.12) | data formatting | bytes 16384
